TPU v7x, 32 devices: a whole 2x2x4 slice. The times are simulated.
32 devices in a mesh: gx: 16 (over z, x, core), gy: 2 (over y).
Axes of the slice: x: 2, y: 2, z: 4, core: 2. Of those that a mesh axis runs over, the one named last changes fastest.
Arguments:
- field: float32 [32, 64, 32, 256], P(None, 'gx', 'gy'), may hold values from -6 to 6
- spec_weight: float32 [2, 32, 32, 32, 32, 32], P(None, None, 'gx', 'gy'), may hold values from -3 to 3
- dw_kernel: float32 [32, 3, 3, 3], replicated, may hold values from -1.25 to 1.25
- point_weight: float32 [32, 32], replicated, may hold values from -1 to 1
- bias: float32 [32], replicated, may hold values from -3 to 3
Outputs:
- evolved: float32 [32, 64, 32, 256], P(None, 'gx', 'gy')
All inputs are finite; a program needn't handle non-finite values.
Results may differ from a plain program's by a relative error of at most 0.00005.
Values sent between devices are 32-bit elements; how exact they have to be, the bound alone decides.
A program may use at most 256 MiB of HBM per device.

v0:
```python
import functools

import jax
import jax.numpy as jnp
import ml_dtypes
import numpy as np
from jax import lax
from jax.experimental import pallas as pl
from jax.experimental.pallas import tpu as pltpu
from jax.sharding import PartitionSpec as P

MIB = 1 << 20


def params(mib, **more):
    return pltpu.CompilerParams(vmem_limit_bytes=mib * MIB, **more)


def halves(a):
    high = a.astype(jnp.bfloat16)
    return high, (a - high.astype(jnp.float32)).astype(jnp.bfloat16)


def left(a, axis):
    high, low = halves(a)
    return jnp.concatenate([high, low, high], axis=axis)


def right(a, axis):
    high, low = halves(a)
    return jnp.concatenate([high, high, low], axis=axis)


def table_halves(a):
    high = a.astype(ml_dtypes.bfloat16)
    return high, (a - high.astype(np.float32)).astype(ml_dtypes.bfloat16)


def table_left(a):
    high, low = table_halves(a)
    return np.concatenate([high, low, high], axis=1)


def table_right(a):
    high, low = table_halves(a)
    return np.concatenate([high, high, low], axis=0)


def dot(a, b, dims=((1,), (0,))):
    return lax.dot_general(a, b, (dims, ((), ())), preferred_element_type=jnp.float32)


def kept(modes, length):
    index = np.arange(modes)
    return np.where(index < modes // 2, index, index + length - modes)


def waves(freqs, length):
    angle = (freqs[:, None] * np.arange(length)[None, :] % length) * (2.0 * np.pi / length)
    return np.cos(angle), np.sin(angle)


def table_pair(modes, length, direction):
    cosine, sine = waves(kept(modes, length), length)
    upper = np.stack([cosine, direction * sine])
    lower = np.stack([-direction * sine, cosine])
    return np.stack([upper, lower])


def rows_z(modes, depth, groups, pieces, table):
    kc = modes // (groups * pieces)
    return table.reshape(2, groups, pieces, kc, depth).transpose(2, 1, 0, 3, 4).reshape(2 * modes, depth).astype(np.float32)


def tables(cfg):
    gx, gy, rx, ry, depth, modes, pieces = cfg
    full_x, full_y = rx * gx, ry * gy
    cosine, sine = waves(np.arange(modes), depth)
    zfwd = rows_z(modes, depth, gy, pieces, np.stack([cosine, -sine]))
    weight = (np.where(np.arange(modes) == 0, 1.0, 2.0) / depth)[:, None]
    zback = rows_z(modes, depth, gy, pieces, np.stack([weight * cosine, -weight * sine]))
    yfwd = table_pair(modes, full_y, 1.0).transpose(2, 0, 1, 3).reshape(2 * modes, 2 * full_y).astype(np.float32)
    yback = (table_pair(modes, full_y, -1.0) / full_y).transpose(3, 0, 2, 1)
    yback = yback.reshape(2 * full_y, 2 * modes).astype(np.float32)
    xtab = table_pair(modes, full_x, 1.0).reshape(2, 2, modes, gx, rx).transpose(4, 1, 3, 0, 2)
    xfwd = np.zeros((rx, 4, 2, gx, 4, 2, modes), np.float32)
    for j in range(4):
        xfwd[:, j, :, :, j] = xtab
    xfwd = xfwd.reshape(rx * 8 * gx, 8 * modes)
    xback = (table_pair(modes, full_x, -1.0) / full_x).reshape(2, 2, modes, gx, rx)
    xback = xback.transpose(4, 0, 3, 1, 2).reshape(rx * 2 * gx, 2 * modes)
    xback = np.repeat(xback, 8, axis=1).astype(np.float32)
    return (table_left(zfwd), table_left(yfwd), table_right(xfwd), table_left(xback), table_left(yback),
            table_right(zback))


def layer_kernel(cfg, zfwd, yfwd, xfwd, xback, yback, zback, dw, pw, bias, field_hbm, weight_hbm, out_hbm,
                 weight, pad, raw, acc, taps, small, point, zs, zr, ys, yr, ms, mr, ts, tr, spec, parts,
                 fsem, wsem, zss, zrs, yss, yrs, mss, mrs, tss, trs, hss, hrs):
    gx, gy, rx, ry, depth, modes, pieces = cfg
    chans = pad.shape[2]
    lanes = rx * chans
    full_y = ry * gy
    nlc, kl = weight.shape[2:4]
    kc = kl // pieces
    quads = kc // 4
    groups = nlc * quads
    xblk = nlc * 2 * kc
    yblk = ry * 2 * kc
    mx, my = lax.axis_index("gx"), lax.axis_index("gy")
    MESH = pl.DeviceIdType.MESH

    def weight_copy(p):
        at = pl.ds(p * kc, kc)
        return pltpu.make_async_copy(weight_hbm.at[:, :, :, at], weight.at[:, :, :, at], wsem.at[p])

    tiles = [(h, x) for x in range(rx) for h in range(depth // 128)]

    def field_copy(i):
        h, x = tiles[i]
        return pltpu.make_async_copy(field_hbm.at[:, x, :, pl.ds(h * 128, 128)], raw.at[h, x], fsem.at[i])

    for i in range(len(tiles)):
        field_copy(i).start()
    for p in range(pieces):
        weight_copy(p).start()

    barrier = pltpu.get_barrier_semaphore()
    for d in range(1, gx):
        pl.semaphore_signal(barrier, inc=1, device_id=(lax.rem(mx + d, gx), my), device_id_type=MESH)
    for d in range(1, gy):
        pl.semaphore_signal(barrier, inc=1, device_id=(mx, lax.rem(my + d, gy)), device_id_type=MESH)

    def block(ref, p, at, rows):
        return ref.at[p, pl.ds(pl.multiple_of(at * rows, 8), rows)]

    def xcopy(src, dst, ssem, rsem, p, i):
        half = (i + 1) // 2
        to = lax.rem(mx + gx // 2 + half * (1 - 2 * lax.rem(i, 2)) + gx, gx)
        return pltpu.make_async_remote_copy(
            src_ref=block(src, p, to, xblk), dst_ref=block(dst, p, mx, xblk), send_sem=ssem.at[p],
            recv_sem=rsem.at[p], device_id=(to, my), device_id_type=MESH)

    def ycopy(src, dst, ssem, rsem, p, d):
        to = lax.rem(my + d + 1, gy)
        return pltpu.make_async_remote_copy(
            src_ref=block(src, p, to, yblk), dst_ref=block(dst, p, my, yblk), send_sem=ssem.at[p],
            recv_sem=rsem.at[p], device_id=(mx, to), device_id_type=MESH)

    def xall(src, dst, ssem, rsem, p):
        rows = pl.ds(0, (gx - 1) * xblk)
        return pltpu.make_async_remote_copy(
            src_ref=src.at[p, rows], dst_ref=dst.at[p, rows], send_sem=ssem.at[p], recv_sem=rsem.at[p],
            device_id=(lax.rem(mx + 1, gx), my), device_id_type=MESH)

    def yall(src, dst, ssem, rsem, p):
        rows = pl.ds(0, (gy - 1) * yblk)
        return pltpu.make_async_remote_copy(
            src_ref=src.at[p, rows], dst_ref=dst.at[p, rows], send_sem=ssem.at[p], recv_sem=rsem.at[p],
            device_id=(mx, lax.rem(my + 1, gy)), device_id_type=MESH)

    def each(make, count, *args):
        def step(i, carry):
            make(*args, i).start()
            return carry
        lax.fori_loop(0, count - 1, step, 0)

    zargs, yargs = (zs, zr, zss, zrs), (ys, yr, yss, yrs)
    margs, targs = (ms, mr, mss, mrs), (ts, tr, tss, trs)

    def keep_own(src, dst, p, at, rows):
        own = pl.ds(pl.multiple_of(at * rows, 8), rows)
        dst[p, own, :] = src[p, own, :]

    def halo(i):
        if i < 2:
            to = lax.rem(mx + (1 if i == 0 else gx - 1), gx)
            src = pad.at[pl.ds(1, ry), pl.ds(rx if i == 0 else 1, 1)]
            dst = pad.at[pl.ds(1, ry), pl.ds(0 if i == 0 else rx + 1, 1)]
            where = (to, my)
        else:
            to = lax.rem(my + (1 if i == 2 else gy - 1), gy)
            src = pad.at[pl.ds(ry if i == 2 else 1, 1)]
            dst = pad.at[pl.ds(0 if i == 2 else ry + 1, 1)]
            where = (mx, to)
        return pltpu.make_async_remote_copy(
            src_ref=src, dst_ref=dst, send_sem=hss.at[i], recv_sem=hrs.at[i], device_id=where, device_id_type=MESH)

    small[...] = jnp.zeros_like(small)
    for i in range(9):
        small[3 * i : 3 * i + 3, :chans] = dw[i // 3, i % 3]
    small[27:28, :chans] = bias[...]
    turned_small = small[...].T
    for i in range(28):
        taps[i] = jnp.broadcast_to(turned_small[:chans, i : i + 1], (chans, 128))
    small[...] = jnp.zeros_like(small)
    for x in range(rx):
        small[x * chans : (x + 1) * chans, x * chans : (x + 1) * chans] = pw[...]
    point[...] = left(small[...].T, 1)

    for i in range(len(tiles)):
        field_copy(i).wait()
    flat = raw.reshape(depth // 128, rx, chans * ry, 128)

    def forward(i, carry):
        data = []
        for yy in range(4):
            y = i * 4 + yy
            for x in range(rx):
                cell = jnp.concatenate(
                    [flat[h, x, pl.ds(y, chans, stride=ry), :] for h in range(depth // 128)], axis=1)
                pad[y + 1, x + 1] = cell
                data.append(cell)
        zspec = dot(zfwd[...], right(jnp.concatenate(data, axis=0), 1), ((1,), (1,)))
        for yy in range(4):
            for p in range(pieces):
                for g in range(gy):
                    at = (p * gy + g) * 2 * kc
                    row = pl.ds(pl.multiple_of((g * ry + i * 4 + yy) * 2 * kc, 8), 2 * kc)
                    zs[p, row, :] = zspec[at : at + 2 * kc, yy * lanes : (yy + 1) * lanes]
        return carry

    lax.fori_loop(0, ry // 4, forward, 0)

    pl.semaphore_wait(barrier, gx + gy - 2)
    for p in range(pieces):
        each(ycopy, gy, *zargs, p)

    def second(p, carry):
        keep_own(zs, zr, p, my, yblk)
        yall(*zargs, p).wait_recv()
        data = jnp.concatenate([
            jnp.concatenate([zr[p, pl.ds(r * kc + k, full_y, stride=2 * kc), :] for r in range(2)], axis=0)
            for k in range(kc)], axis=1)
        yspec = dot(yfwd[...], right(data, 0))
        for k in range(kc):
            ys[p, pl.ds(k, 2 * modes, stride=kc), :] = yspec[:, k * lanes : (k + 1) * lanes]
        each(xcopy, gx, *yargs, p)
        keep_own(ys, yr, p, mx, xblk)
        return carry

    lax.fori_loop(0, pieces, second, 0)

    def local_part(y, carry):
        here = pad[y + 1, pl.ds(1, rx)].reshape(lanes, depth)
        base = dot(point[...], right(here, 0))
        for cc in range(0, chans, 8):
            sums = [[None] * 3 for _ in range(rx)]
            for b in range(3):
                for xp in range(rx + 2):
                    value = pad[y + b, xp, cc : cc + 8, :]
                    for a in range(3):
                        x = xp - a
                        if 0 <= x < rx:
                            for e in range(3):
                                tap = taps[(a * 3 + b) * 3 + e, cc : cc + 8, :]
                                term = jnp.concatenate([tap] * (depth // 128), axis=1) * value
                                sums[x][e] = term if sums[x][e] is None else sums[x][e] + term
            shift = jnp.concatenate([taps[27, cc : cc + 8, :]] * (depth // 128), axis=1)
            for x in range(rx):
                total = sums[x][1] + pltpu.roll(sums[x][0], 1, 1) + pltpu.roll(sums[x][2], depth - 1, 1)
                acc[y, x, cc : cc + 8, :] = total + base[x * chans + cc : x * chans + cc + 8, :] + shift
        return carry

    def channels(p, before):
        xall(*yargs, p).wait_recv()

        @pl.when(p == 0)
        def _():
            halo(0).start()
            halo(1).start()

        gathered = []
        for g in range(groups):
            nl, q = g // quads, g % quads
            data = jnp.concatenate(
                [yr[p, pl.ds((nl * 2 + s) * kc + q * 4 + j, gx, stride=xblk), :] for j in range(4) for s in range(2)],
                axis=0)
            turned = data.T
            gathered.append(jnp.concatenate([turned[x * chans : (x + 1) * chans] for x in range(rx)], axis=1))
        spec[...] = dot(left(jnp.concatenate(gathered, axis=0), 1), xfwd[...])
        weight_copy(p).wait()

        def mix(g, carry):
            nl, q = g // quads, g % quads
            at = pl.ds(pl.multiple_of(g * chans, 8), chans)
            for m in range(modes):
                res, ims = [], []
                for j in range(4):
                    lane = j * 2 * modes + m
                    half = spec[at, j * 2 * modes // 128 * 128 : j * 2 * modes // 128 * 128 + 128]
                    lane = lane % 128
                    re = jnp.broadcast_to(half[:, lane : lane + 1], (chans, chans))
                    im = jnp.broadcast_to(half[:, lane + modes : lane + modes + 1], (chans, chans))
                    wre = weight[0, m, nl, p * kc + q * 4 + j]
                    wim = weight[1, m, nl, p * kc + q * 4 + j]
                    mre = re * wre - im * wim
                    mim = re * wim + im * wre
                    res.append(sum(mre[i : i + 8] for i in range(8, chans, 8)) + mre[:8])
                    ims.append(sum(mim[i : i + 8] for i in range(8, chans, 8)) + mim[:8])
                parts[g, m * 8 : m * 8 + 8, :] = jnp.concatenate(res, axis=1)
                parts[g, (modes + m) * 8 : (modes + m) * 8 + 8, :] = jnp.concatenate(ims, axis=1)
            return carry

        lax.fori_loop(0, groups, mix, 0)
        back = dot(xback[...], right(jnp.concatenate([parts[g] for g in range(groups)], axis=1), 0))
        for g in range(groups):
            nl, q = g // quads, g % quads
            for j in range(4):
                lane = g * 128 + j * chans
                for s in range(2):
                    ms[p, pl.ds((nl * 2 + s) * kc + q * 4 + j, gx, stride=xblk), :] = jnp.concatenate(
                        [back[(x * 2 + s) * gx : (x * 2 + s + 1) * gx, lane : lane + chans] for x in range(rx)], axis=1)
        each(xcopy, gx, *margs, p)
        keep_own(ms, mr, p, mx, xblk)

        @pl.when(p == 0)
        def _():
            halo(0).wait_recv()
            halo(1).wait_recv()
            halo(2).start()
            halo(3).start()

        return before

    lax.fori_loop(0, pieces, channels, 0)

    halo(2).wait_recv()
    halo(3).wait_recv()
    lax.fori_loop(0, ry, local_part, 0)

    def second_back(p, carry):
        xall(*margs, p).wait_recv()
        data = jnp.concatenate([mr[p, pl.ds(k, 2 * modes, stride=kc), :] for k in range(kc)], axis=1)
        tall = dot(yback[...], right(data, 0))
        for k in range(kc):
            ts[p, pl.ds(k, 2 * full_y, stride=kc), :] = tall[:, k * lanes : (k + 1) * lanes]
        each(ycopy, gy, *targs, p)
        keep_own(ts, tr, p, my, yblk)
        return carry

    lax.fori_loop(0, pieces, second_back, 0)
    for p in range(pieces):
        yall(*targs, p).wait_recv()

    def finish(i, carry):
        data = jnp.concatenate([
            jnp.concatenate([
                tr[p, pl.ds(pl.multiple_of((g * ry + i * 4 + yy) * 2 * kc, 8), 2 * kc), :]
                for p in range(pieces) for g in range(gy)], axis=0)
            for yy in range(4)], axis=1)
        spectral = dot(left(data, 0), zback[...], ((0,), (0,)))
        for yy in range(4):
            y = i * 4 + yy
            for x in range(rx):
                at = yy * lanes + x * chans
                total = spectral[at : at + chans] + acc[y, x]
                for h in range(depth // 128):
                    flat[h, x, pl.ds(y, chans, stride=ry), :] = total[:, h * 128 : (h + 1) * 128]
        return carry

    lax.fori_loop(0, ry // 4, finish, 0)

    def out_copy(i):
        h, x = tiles[i]
        return pltpu.make_async_copy(raw.at[h, x], out_hbm.at[:, x, :, pl.ds(h * 128, 128)], fsem.at[i])

    for i in range(len(tiles)):
        out_copy(i).start()
    for i in range(4):
        halo(i).wait_send()
    for p in range(pieces):
        yall(*zargs, p).wait_send()
        xall(*yargs, p).wait_send()
        xall(*margs, p).wait_send()
        yall(*targs, p).wait_send()
    for i in range(len(tiles)):
        out_copy(i).wait()


def on_device(field, spec_weight, dw_kernel, point_weight, bias):
    gx, gy = lax.axis_size("gx"), lax.axis_size("gy")
    chans, rx, ry, depth = field.shape
    modes, nlc, kl = spec_weight.shape[1:4]
    lanes = rx * chans
    f32 = jnp.float32
    pieces = 2 if kl % 8 == 0 else 1
    kc = kl // pieces
    cfg = (gx, gy, rx, ry, depth, modes, pieces)

    vmem = pl.BlockSpec(memory_space=pltpu.VMEM)
    hbm = pl.BlockSpec(memory_space=pl.ANY)
    ybuf = pltpu.VMEM((pieces, gy * ry * 2 * kc, lanes), f32)
    xbuf = pltpu.VMEM((pieces, gx * nlc * 2 * kc, lanes), f32)
    dma = pltpu.SemaphoreType.DMA
    out = pl.pallas_call(
        functools.partial(layer_kernel, cfg),
        in_specs=[vmem] * 9 + [hbm] * 2,
        out_specs=hbm,
        out_shape=jax.ShapeDtypeStruct(field.shape, f32),
        scratch_shapes=[
            pltpu.VMEM(spec_weight.shape, f32),
            pltpu.VMEM((ry + 2, rx + 2, chans, depth), f32),
            pltpu.VMEM((depth // 128, rx, chans, ry, 128), f32),
            pltpu.VMEM((ry, rx, chans, depth), f32),
            pltpu.VMEM((28, chans, 128), f32),
            pltpu.VMEM((lanes, lanes), f32),
            pltpu.VMEM((lanes, 3 * lanes), jnp.bfloat16),
            ybuf, ybuf, xbuf, xbuf, xbuf, xbuf, ybuf, ybuf,
            pltpu.VMEM((nlc * kc // 4 * chans, 8 * modes), f32),
            pltpu.VMEM((nlc * kc // 4, 16 * modes, 128), f32),
            dma((rx * depth // 128,)), dma((pieces,)),
            dma((pieces,)), dma((pieces,)), dma((pieces,)), dma((pieces,)),
            dma((pieces,)), dma((pieces,)), dma((pieces,)), dma((pieces,)),
            dma((4,)), dma((4,)),
        ],
        compiler_params=params(60, collective_id=0, has_side_effects=True),
        name="layer",
    )(*tables(cfg), jnp.transpose(dw_kernel, (1, 2, 3, 0)), point_weight, bias[None], field, spec_weight)
    return jax.nn.gelu(out)


def solution(mesh):
    placed = (P(None, "gx", "gy", None), P(None, None, "gx", "gy", None, None), P(), P(), P())
    return jax.shard_map(
        on_device, mesh=mesh, in_specs=placed, out_specs=P(None, "gx", "gy", None), check_vma=False
    )
```

profile of v0, /device:TPU:0, one launch (start us, length us, event | category | flops | bytes accessed | tf_op | source)
XLA Modules:
  0.0 74.8 jit_solution(4601743951745087989)
XLA Ops:
  0.0 71.3 %layer.1 = f32[32,4,16,256]{3,2,1,0:T(8,128)} custom-call(bf16[64,768]{1,0:T(8,128)(2,1)} %constant.20.clone.zfwd, bf16[64,192]{1,0:T(8,128)(2,1)} %constant.21.clone.yfwd, bf16[1536,256]{1,0:T(8,128)(2,1)} %constant.22.clone.xfwd, bf16[128,1536]{1,0:T(8,128)(2,1)} %constant.23.clone.xback, bf16[64,192]{1,0:T(8,128)(2,1)} %constant.24.clone.yback, ...), custom_call_target="tpu_custom_call" | custom-call | tf_op jit(solution)/shard_map/layer/pallas_call | solution.py:396
  71.3 3.5 %fusion.6 = f32[32,4,16,256]{3,2,1,0:T(8,128)} fusion(f32[32,4,16,256]{3,2,1,0:T(8,128)} %layer.1), kind=kLoop, calls=%fused_computation.7 | loop fusion | flops 4194304 | bytes 4194304 | tf_op jit(solution)/shard_map/mul | solution.py:420
where the time goes:
time: 75.5 us; the launch traced here: 74.8 us
  Pallas kernels  71.3 us (94%)
  other arithmetic  3.53 us (5%)
    pallas_call x1, Pallas kernels, on_device(): pl.pallas_call(functools.partial(layer_kernel, cfg), in_specs=[vmem] * 9...  71.3 us
    mul x1, other arithmetic, on_device(): return jax.nn.gelu(out)  3.53 us

commit v1 on v0

--- a/solution.py
+++ b/solution.py
@@ -82,15 +82,16 @@
     yfwd = table_pair(modes, full_y, 1.0).transpose(2, 0, 1, 3).reshape(2 * modes, 2 * full_y).astype(np.float32)
     yback = (table_pair(modes, full_y, -1.0) / full_y).transpose(3, 0, 2, 1)
     yback = yback.reshape(2 * full_y, 2 * modes).astype(np.float32)
-    xtab = table_pair(modes, full_x, 1.0).reshape(2, 2, modes, gx, rx).transpose(4, 1, 3, 0, 2)
-    xfwd = np.zeros((rx, 4, 2, gx, 4, 2, modes), np.float32)
+    xtab = table_pair(modes, full_x, 1.0).reshape(2, 2, modes, gx, rx)
+    factor = np.stack([np.stack([xtab[0], xtab[1]]), np.stack([-xtab[1], xtab[0]])])
+    xfwd = factor.transpose(0, 3, 1, 5, 2, 4).reshape(4 * modes, rx * 2 * gx)
+    xfwd = np.repeat(xfwd, 4, axis=0)
+    xtab = (table_pair(modes, full_x, -1.0) / full_x).reshape(2, 2, modes, gx, rx).transpose(4, 0, 3, 2, 1)
+    xback = np.zeros((4, rx, 2, gx, modes, 2, 4), np.float32)
     for j in range(4):
-        xfwd[:, j, :, :, j] = xtab
-    xfwd = xfwd.reshape(rx * 8 * gx, 8 * modes)
-    xback = (table_pair(modes, full_x, -1.0) / full_x).reshape(2, 2, modes, gx, rx)
-    xback = xback.transpose(4, 0, 3, 1, 2).reshape(rx * 2 * gx, 2 * modes)
-    xback = np.repeat(xback, 8, axis=1).astype(np.float32)
-    return (table_left(zfwd), table_left(yfwd), table_right(xfwd), table_left(xback), table_left(yback),
+        xback[j, ..., j] = xtab
+    xback = xback.reshape(4 * rx * 2 * gx, 8 * modes)
+    return (table_left(zfwd), table_left(yfwd), table_left(xfwd), table_left(xback), table_left(yback),
             table_right(zback))
 
 
@@ -273,33 +274,35 @@
         gathered = []
         for g in range(groups):
             nl, q = g // quads, g % quads
-            data = jnp.concatenate(
-                [yr[p, pl.ds((nl * 2 + s) * kc + q * 4 + j, gx, stride=xblk), :] for j in range(4) for s in range(2)],
-                axis=0)
-            turned = data.T
-            gathered.append(jnp.concatenate([turned[x * chans : (x + 1) * chans] for x in range(rx)], axis=1))
-        spec[...] = dot(left(jnp.concatenate(gathered, axis=0), 1), xfwd[...])
+            data = [
+                jnp.concatenate(
+                    [yr[p, pl.ds((nl * 2 + s) * kc + q * 4 + j, gx, stride=xblk), :] for s in range(2)], axis=0)
+                for j in range(4)]
+            gathered.append(jnp.concatenate([
+                jnp.concatenate([part[:, x * chans : (x + 1) * chans] for part in data], axis=1)
+                for x in range(rx)], axis=0))
+        wide = dot(xfwd[...], right(jnp.concatenate(gathered, axis=1), 0))
+        span = 4 * chans
+        shape = (8 * modes, span)
+        own = lax.rem(lax.broadcasted_iota(jnp.int32, shape, 0), 4) == lax.broadcasted_iota(jnp.int32, shape, 1) // chans
+        for g in range(groups):
+            for r in range(2):
+                kept_part = jnp.where(own, wide[r * 8 * modes : (r + 1) * 8 * modes, g * span : (g + 1) * span], 0.0)
+                high = kept_part.astype(jnp.bfloat16).astype(jnp.float32)
+                both = jnp.concatenate(
+                    [high.reshape(modes, 8, span), (kept_part - high).reshape(modes, 8, span)], axis=1)
+                spec[g, :, r * span : (r + 1) * span] = both.reshape(16 * modes, span).astype(jnp.bfloat16)
         weight_copy(p).wait()
 
         def mix(g, carry):
             nl, q = g // quads, g % quads
-            at = pl.ds(pl.multiple_of(g * chans, 8), chans)
             for m in range(modes):
-                res, ims = [], []
-                for j in range(4):
-                    lane = j * 2 * modes + m
-                    half = spec[at, j * 2 * modes // 128 * 128 : j * 2 * modes // 128 * 128 + 128]
-                    lane = lane % 128
-                    re = jnp.broadcast_to(half[:, lane : lane + 1], (chans, chans))
-                    im = jnp.broadcast_to(half[:, lane + modes : lane + modes + 1], (chans, chans))
-                    wre = weight[0, m, nl, p * kc + q * 4 + j]
-                    wim = weight[1, m, nl, p * kc + q * 4 + j]
-                    mre = re * wre - im * wim
-                    mim = re * wim + im * wre
-                    res.append(sum(mre[i : i + 8] for i in range(8, chans, 8)) + mre[:8])
-                    ims.append(sum(mim[i : i + 8] for i in range(8, chans, 8)) + mim[:8])
-                parts[g, m * 8 : m * 8 + 8, :] = jnp.concatenate(res, axis=1)
-                parts[g, (modes + m) * 8 : (modes + m) * 8 + 8, :] = jnp.concatenate(ims, axis=1)
+                block_w = jnp.concatenate(
+                    [weight[r, m, nl, p * kc + q * 4 + j] for r in range(2) for j in range(4)], axis=0)
+                high, low = halves(block_w)
+                rows = spec[g, m * 16 : (m + 1) * 16, :]
+                total = dot(jnp.concatenate([rows, rows], axis=1), jnp.concatenate([high, low], axis=0))
+                parts[g, m * 8 : (m + 1) * 8, :] = total[:8] + total[8:]
             return carry
 
         lax.fori_loop(0, groups, mix, 0)
@@ -307,10 +310,11 @@
         for g in range(groups):
             nl, q = g // quads, g % quads
             for j in range(4):
-                lane = g * 128 + j * chans
                 for s in range(2):
+                    at = (j * rx * 2 + s) * gx
                     ms[p, pl.ds((nl * 2 + s) * kc + q * 4 + j, gx, stride=xblk), :] = jnp.concatenate(
-                        [back[(x * 2 + s) * gx : (x * 2 + s + 1) * gx, lane : lane + chans] for x in range(rx)], axis=1)
+                        [back[at + x * 2 * gx : at + (x * 2 + 1) * gx, g * chans : (g + 1) * chans]
+                         for x in range(rx)], axis=1)
         each(xcopy, gx, *margs, p)
         keep_own(ms, mr, p, mx, xblk)
 
@@ -407,8 +411,8 @@
             pltpu.VMEM((lanes, lanes), f32),
             pltpu.VMEM((lanes, 3 * lanes), jnp.bfloat16),
             ybuf, ybuf, xbuf, xbuf, xbuf, xbuf, ybuf, ybuf,
-            pltpu.VMEM((nlc * kc // 4 * chans, 8 * modes), f32),
-            pltpu.VMEM((nlc * kc // 4, 16 * modes, 128), f32),
+            pltpu.VMEM((nlc * kc // 4, 16 * modes, 8 * chans), jnp.bfloat16),
+            pltpu.VMEM((nlc * kc // 4, 8 * modes, chans), f32),
             dma((rx * depth // 128,)), dma((pieces,)),
             dma((pieces,)), dma((pieces,)), dma((pieces,)), dma((pieces,)),
             dma((pieces,)), dma((pieces,)), dma((pieces,)), dma((pieces,)),

time: 75.5 us -> 63.7 us (0.84)
  the two profiles are of different devices: /device:TPU:0 before, /device:TPU:17 now
where the time goes in v1:
time: 63.7 us; the launch traced here: 63.5 us
  Pallas kernels  60 us (94%)
  other arithmetic  3.53 us (6%)
    pallas_call x1, Pallas kernels, on_device(): pl.pallas_call(functools.partial(layer_kernel, cfg), in_specs=[vmem] * 9...  60 us
    mul x1, other arithmetic, on_device(): return jax.nn.gelu(out)  3.53 us

profile of v1, /device:TPU:17, one launch (start us, length us, event | category | flops | bytes accessed | tf_op | source)
XLA Modules:
  0.0 63.5 jit_solution(3818471692094123416)
XLA Ops:
  0.0 60.0 %layer.1 = f32[32,4,16,256]{3,2,1,0:T(8,128)} custom-call(bf16[64,768]{1,0:T(8,128)(2,1)} %constant.20.clone.zfwd, bf16[64,192]{1,0:T(8,128)(2,1)} %constant.21.clone.yfwd, bf16[512,384]{1,0:T(8,128)(2,1)} %constant.22.clone.xfwd, bf16[512,768]{1,0:T(8,128)(2,1)} %constant.23.clone.xback, bf16[64,192]{1,0:T(8,128)(2,1)} %constant.24.clone.yback, ...), custom_call_target="tpu_custom_call" | custom-call | tf_op jit(solution)/shard_map/layer/pallas_call | solution.py:400
  60.0 3.5 %fusion.6 = f32[32,4,16,256]{3,2,1,0:T(8,128)} fusion(f32[32,4,16,256]{3,2,1,0:T(8,128)} %layer.1), kind=kLoop, calls=%fused_computation.7 | loop fusion | flops 4194304 | bytes 4194304 | tf_op jit(solution)/shard_map/mul | solution.py:424

commit v2 on v1

--- a/solution.py
+++ b/solution.py
@@ -96,7 +96,7 @@
 
 
 def layer_kernel(cfg, zfwd, yfwd, xfwd, xback, yback, zback, dw, pw, bias, field_hbm, weight_hbm, out_hbm,
-                 weight, pad, raw, acc, taps, small, point, zs, zr, ys, yr, ms, mr, ts, tr, spec, parts,
+                 weight, pad, raw, edges, acc, taps, small, point, zs, zr, ys, yr, ms, mr, ts, tr, spec, parts,
                  fsem, wsem, zss, zrs, yss, yrs, mss, mrs, tss, trs, hss, hrs):
     gx, gy, rx, ry, depth, modes, pieces = cfg
     chans = pad.shape[2]
@@ -176,8 +176,8 @@
     def halo(i):
         if i < 2:
             to = lax.rem(mx + (1 if i == 0 else gx - 1), gx)
-            src = pad.at[pl.ds(1, ry), pl.ds(rx if i == 0 else 1, 1)]
-            dst = pad.at[pl.ds(1, ry), pl.ds(0 if i == 0 else rx + 1, 1)]
+            src = raw.at[:, rx - 1 if i == 0 else 0]
+            dst = edges.at[i]
             where = (to, my)
         else:
             to = lax.rem(my + (1 if i == 2 else gy - 1), gy)
@@ -201,6 +201,9 @@
 
     for i in range(len(tiles)):
         field_copy(i).wait()
+    pl.semaphore_wait(barrier, gx + gy - 2)
+    halo(0).start()
+    halo(1).start()
     flat = raw.reshape(depth // 128, rx, chans * ry, 128)
 
     def forward(i, carry):
@@ -223,7 +226,6 @@
 
     lax.fori_loop(0, ry // 4, forward, 0)
 
-    pl.semaphore_wait(barrier, gx + gy - 2)
     for p in range(pieces):
         each(ycopy, gy, *zargs, p)
 
@@ -241,6 +243,20 @@
         return carry
 
     lax.fori_loop(0, pieces, second, 0)
+
+    for i in range(2):
+        halo(i).wait_recv()
+    flat_edges = edges.reshape(2, depth // 128, chans * ry, 128)
+
+    def sides(y, carry):
+        for i in range(2):
+            pad[y + 1, 0 if i == 0 else rx + 1] = jnp.concatenate(
+                [flat_edges[i, h, pl.ds(y, chans, stride=ry), :] for h in range(depth // 128)], axis=1)
+        return carry
+
+    lax.fori_loop(0, ry, sides, 0)
+    halo(2).start()
+    halo(3).start()
 
     def local_part(y, carry):
         here = pad[y + 1, pl.ds(1, rx)].reshape(lanes, depth)
@@ -263,14 +279,10 @@
                 acc[y, x, cc : cc + 8, :] = total + base[x * chans + cc : x * chans + cc + 8, :] + shift
         return carry
 
+    lax.fori_loop(1, ry // 2, local_part, 0)
+
     def channels(p, before):
         xall(*yargs, p).wait_recv()
-
-        @pl.when(p == 0)
-        def _():
-            halo(0).start()
-            halo(1).start()
-
         gathered = []
         for g in range(groups):
             nl, q = g // quads, g % quads
@@ -317,21 +329,15 @@
                          for x in range(rx)], axis=1)
         each(xcopy, gx, *margs, p)
         keep_own(ms, mr, p, mx, xblk)
-
-        @pl.when(p == 0)
-        def _():
-            halo(0).wait_recv()
-            halo(1).wait_recv()
-            halo(2).start()
-            halo(3).start()
-
         return before
 
     lax.fori_loop(0, pieces, channels, 0)
 
     halo(2).wait_recv()
     halo(3).wait_recv()
-    lax.fori_loop(0, ry, local_part, 0)
+    lax.fori_loop(ry // 2, ry + 1, lambda y, carry: local_part(lax.rem(y, ry), carry), 0)
+    for i in range(2):
+        halo(i).wait_send()
 
     def second_back(p, carry):
         xall(*margs, p).wait_recv()
@@ -371,7 +377,7 @@
 
     for i in range(len(tiles)):
         out_copy(i).start()
-    for i in range(4):
+    for i in range(2, 4):
         halo(i).wait_send()
     for p in range(pieces):
         yall(*zargs, p).wait_send()
@@ -406,6 +412,7 @@
             pltpu.VMEM(spec_weight.shape, f32),
             pltpu.VMEM((ry + 2, rx + 2, chans, depth), f32),
             pltpu.VMEM((depth // 128, rx, chans, ry, 128), f32),
+            pltpu.VMEM((2, depth // 128, chans, ry, 128), f32),
             pltpu.VMEM((ry, rx, chans, depth), f32),
             pltpu.VMEM((28, chans, 128), f32),
             pltpu.VMEM((lanes, lanes), f32),

time: 63.7 us -> 54.7 us (0.86)
  the two profiles are of different devices: /device:TPU:17 before, /device:TPU:0 now
where the time goes in v2:
time: 54.7 us; the launch traced here: 54.5 us
  Pallas kernels  51 us (93%)
  other arithmetic  3.53 us (6%)
    pallas_call x1, Pallas kernels, on_device(): pl.pallas_call(functools.partial(layer_kernel, cfg), in_specs=[vmem] * 9...  51 us
    mul x1, other arithmetic, on_device(): return jax.nn.gelu(out)  3.53 us

profile of v2, /device:TPU:0, one launch (start us, length us, event | category | flops | bytes accessed | tf_op | source)
XLA Modules:
  0.0 54.5 jit_solution(1962949549583099340)
XLA Ops:
  0.0 51.0 %layer.1 = f32[32,4,16,256]{3,2,1,0:T(8,128)} custom-call(bf16[64,768]{1,0:T(8,128)(2,1)} %constant.20.clone.zfwd, bf16[64,192]{1,0:T(8,128)(2,1)} %constant.21.clone.yfwd, bf16[512,384]{1,0:T(8,128)(2,1)} %constant.22.clone.xfwd, bf16[512,768]{1,0:T(8,128)(2,1)} %constant.23.clone.xback, bf16[64,192]{1,0:T(8,128)(2,1)} %constant.24.clone.yback, ...), custom_call_target="tpu_custom_call" | custom-call | tf_op jit(solution)/shard_map/layer/pallas_call | solution.py:406
  51.0 3.5 %fusion.6 = f32[32,4,16,256]{3,2,1,0:T(8,128)} fusion(f32[32,4,16,256]{3,2,1,0:T(8,128)} %layer.1), kind=kLoop, calls=%fused_computation.7 | loop fusion | flops 4194304 | bytes 4194304 | tf_op jit(solution)/shard_map/mul | solution.py:431

commit v3 on v2

--- a/solution.py
+++ b/solution.py
@@ -394,7 +394,7 @@
     modes, nlc, kl = spec_weight.shape[1:4]
     lanes = rx * chans
     f32 = jnp.float32
-    pieces = 2 if kl % 8 == 0 else 1
+    pieces = 4 if kl % 16 == 0 else 2 if kl % 8 == 0 else 1
     kc = kl // pieces
     cfg = (gx, gy, rx, ry, depth, modes, pieces)
 

time: 54.7 us -> 54.5 us (level)
  the two profiles are of different devices: /device:TPU:0 before, /device:TPU:1 now
where the time goes in v3:
time: 54.5 us; the launch traced here: 54.4 us
  Pallas kernels  50.8 us (93%)
  other arithmetic  3.53 us (6%)
    pallas_call x1, Pallas kernels, on_device(): pl.pallas_call(functools.partial(layer_kernel, cfg), in_specs=[vmem] * 9...  50.8 us
    mul x1, other arithmetic, on_device(): return jax.nn.gelu(out)  3.53 us

profile of v3, /device:TPU:1, one launch (start us, length us, event | category | flops | bytes accessed | tf_op | source)
XLA Modules:
  0.0 54.4 jit_solution(900920756399381397)
XLA Ops:
  0.0 50.8 %layer.1 = f32[32,4,16,256]{3,2,1,0:T(8,128)} custom-call(bf16[64,768]{1,0:T(8,128)(2,1)} %constant.20.clone.zfwd, bf16[64,192]{1,0:T(8,128)(2,1)} %constant.21.clone.yfwd, bf16[512,384]{1,0:T(8,128)(2,1)} %constant.22.clone.xfwd, bf16[512,768]{1,0:T(8,128)(2,1)} %constant.23.clone.xback, bf16[64,192]{1,0:T(8,128)(2,1)} %constant.24.clone.yback, ...), custom_call_target="tpu_custom_call" | custom-call | tf_op jit(solution)/shard_map/layer/pallas_call | solution.py:406
  50.8 3.5 %fusion.6 = f32[32,4,16,256]{3,2,1,0:T(8,128)} fusion(f32[32,4,16,256]{3,2,1,0:T(8,128)} %layer.1), kind=kLoop, calls=%fused_computation.7 | loop fusion | flops 4194304 | bytes 4194304 | tf_op jit(solution)/shard_map/mul | solution.py:431
